TPU v7x, 256 devices: a whole 4x4x8 slice. The times are simulated.
256 devices in a mesh: freq: 32 (over z_hi, x, core), src: 8 (over z_lo, y).
Axes of the slice: x: 4, y: 4, z: 8 (z_hi: 4, z_lo: 2; z = z_hi * 2 + z_lo), core: 2. Of those that a mesh axis runs over, the one named last changes fastest.
Arguments:
- reflection: float32 [2, 256, 1024, 1024], P(None, 'freq', 'src'), as said below
- focusing: float32 [2, 256, 64, 1024], P(None, 'freq', None, 'src'), may hold values from -6 to 6
- onsets: int32 [64, 1024], P('freq', 'src'), may hold values from 1 to 128
Outputs:
- downgoing: float32 [2, 256, 64, 1024], P(None, 'freq', None, 'src')
- upgoing: float32 [2, 256, 64, 1024], P(None, 'freq', None, 'src')
Inputs may be any that keep to these rules, and one draw needn't show every extreme that they name: reflection[c, f, s, r] equals reflection[c, f, r, s] (reciprocity).
All inputs are finite; a program needn't handle non-finite values.
Results may differ from a plain program's by a relative error of at most 0.00014.
Values sent between devices are 32-bit elements; how exact they have to be, the bound alone decides.
A program may use at most 64 MiB of HBM per device.

v0:
```python
import math

import jax
import jax.numpy as jnp
from jax import lax
from jax.sharding import PartitionSpec as P

ITERS = 2


def dft_tables(length):
    samples = jnp.arange(length, dtype=jnp.int32)
    phases = samples[:, None] * samples[None, :] % length
    phase_angles = phases.astype(jnp.float32) * (2.0 * math.pi / length)
    return (jnp.cos(phase_angles), jnp.sin(phase_angles))


def transform(table, sample_values):
    return jnp.einsum("tf,fpx->tpx", table, sample_values, precision=lax.Precision.HIGHEST)


def product(layout_kind, left, right):
    return jnp.einsum(layout_kind, left, right, precision=lax.Precision.HIGHEST)


def windowed(spectra, onsets):
    timed = lax.all_to_all(spectra, "freq", split_axis=2, concat_axis=1, tiled=True)
    length = timed.shape[1]
    cosine_lookup, sin_table = dft_tables(length)
    real_part, imag_part = (timed[0], timed[1])
    time_real = (transform(cosine_lookup, real_part) - transform(sin_table, imag_part)) / length
    time_imag = (transform(sin_table, real_part) + transform(cosine_lookup, imag_part)) / length
    samples = jnp.arange(length, dtype=jnp.int32)
    nearest = jnp.minimum(samples, length - samples)
    kept_mask = (nearest[:, None, None] < onsets[None]).astype(jnp.float32)
    time_real = time_real * kept_mask
    time_imag = time_imag * kept_mask
    back_real = transform(cosine_lookup, time_real) + transform(sin_table, time_imag)
    back_imag = transform(cosine_lookup, time_imag) - transform(sin_table, time_real)
    return lax.all_to_all(
        jnp.stack([back_real, back_imag]), "freq", split_axis=1, concat_axis=2, tiled=True
    )


def per_device(reflection, focusing, onsets):
    refl_real, refl_imag = (reflection[0], reflection[1])
    downgoing = focusing
    upgoing = focusing
    for iteration in range(ITERS):
        fragment_list = lax.all_gather(downgoing, "src", axis=3, tiled=True)
        layout_kind = "idt,iqt->iqd"
        add_real = product(layout_kind, reflection[0], fragment_list[0]) - product(
            layout_kind, reflection[1], fragment_list[1]
        )
        add_imag = product(layout_kind, reflection[0], fragment_list[1]) + product(
            layout_kind, reflection[1], fragment_list[0]
        )
        forward = jnp.stack([add_real, add_imag])
        upgoing = windowed(forward, onsets)
        layout_kind = "jkn,juk->jun"
        running_real_total = product(layout_kind, refl_real, upgoing[0]) + product(
            layout_kind, refl_imag, upgoing[1]
        )
        partial_imag = product(layout_kind, refl_real, upgoing[1]) - product(
            layout_kind, refl_imag, upgoing[0]
        )
        adjoint = lax.psum_scatter(
            jnp.stack([running_real_total, partial_imag]), "src", scatter_dimension=3, tiled=True
        )
        downgoing = focusing - windowed(adjoint, onsets)
    return (downgoing, upgoing)


def solution(mesh):
    placed = (P(None, "freq", "src", None), P(None, "freq", None, "src"), P("freq", "src"))
    return jax.shard_map(
        per_device,
        mesh=mesh,
        in_specs=placed,
        out_specs=(P(None, "freq", None, "src"), P(None, "freq", None, "src")),
        check_vma=False,
    )
```

profile of v0, /device:TPU:1, one launch (start us, length us, event | category | flops | bytes accessed | tf_op | source)
XLA Modules:
  0.0 573.7 jit_solution(2177541047710664736)
XLA Ops:
  7.9 66.5 %all-gather.3.cloned.1.call-done = f32[2,8,64,1024]{3,2,1,0:T(8,128)} async-done(((f32[2,8,64,128]{3,2,1,0:T(8,128)}), f32[2,8,64,1024]{3,2,1,0:T(8,128)}) %all-gather.3.cloned.1.call-update) | async-done | bytes 4194320 | tf_op jit(solution)/shard_map/all_gather | solution.py:50
  74.4 7.4 %fusion.12 = f32[8,64,128]{2,1,0:T(8,128)S(1)} fusion(f32[2,8,128,1024]{3,2,1,0:T(8,128)} %param.3, f32[2,8,64,1024]{3,2,1,0:T(8,128)} %all-gather.3.cloned.1.call-done), kind=kOutput, calls=%fused_computation.14 | convolution fusion | flops 805306368 | bytes 6553600 | tf_op jit(solution)/shard_map/idt,iqt->iqd/dot_general | solution.py:23
  81.8 7.4 %fusion.14 = f32[8,64,128]{2,1,0:T(8,128)S(1)} fusion(f32[2,8,128,1024]{3,2,1,0:T(8,128)} %param.3, f32[2,8,64,1024]{3,2,1,0:T(8,128)} %all-gather.3.cloned.1.call-done), kind=kOutput, calls=%fused_computation.16 | convolution fusion | flops 805306368 | bytes 6553600 | tf_op jit(solution)/shard_map/idt,iqt->iqd/dot_general | solution.py:23
  89.3 4.5 fusion.65
  93.7 4.9 fusion.59
  99.8 11.8 %all-to-all-start = ((f32[2,8,64,128]{3,1,0,2:T(8,128)}), f32[2,8,64,128]{3,1,0,2:T(8,128)S(1)}, u32[]{:S(2)}, u32[]{:S(2)}) async-start(f32[2,8,64,128]{3,1,0,2:T(8,128)} %copy.20), calls=%async_computation | async-start | bytes 1048576 | tf_op jit(solution)/shard_map/all_to_all | solution.py:27
  111.6 18.3 %all-to-all-done = f32[2,8,64,128]{3,1,0,2:T(8,128)S(1)} async-done(((f32[2,8,64,128]{3,1,0,2:T(8,128)}), f32[2,8,64,128]{3,1,0,2:T(8,128)S(1)}, u32[]{:S(2)}, u32[]{:S(2)}) %all-to-all-start) | async-done | bytes 524320 | tf_op jit(solution)/shard_map/all_to_all | solution.py:27
  130.0 1.4 fusion.124
  131.3 1.4 fusion.153
  132.7 1.4 fusion.97
  134.1 1.6 fusion.148
  135.7 1.4 fusion.96
  137.1 1.6 fusion.151
  138.7 1.6 fusion.92
  140.3 1.6 fusion.93
  142.4 22.8 %all_to_all.129 = f32[2,256,2,128]{3,2,0,1:T(2,128)S(1)} all-to-all(f32[2,256,2,128]{3,2,0,1:T(2,128)S(1)} %copy.22), channel_id=1, replica_groups=mesh['freq'=32,'src'=8] {'freq'}, dimensions={1} | all-to-all | bytes 1048576 | tf_op jit(solution)/shard_map/all_to_all | solution.py:40
  165.5 2.4 fusion.8
  167.9 2.4 fusion.10
  170.3 2.4 subtract_bitcast_fusion.1
  172.7 2.4 add_bitcast_fusion.1
  175.2 2.3 pad_maximum_fusion
  177.5 50.5 %reduce-scatter.3.cloned.1.call-done = f32[2,8,64,128]{3,2,1,0:T(8,128)} async-done(((f32[2,8,64,1024]{3,2,1,0:T(8,128)}), f32[2,8,64,128]{3,2,1,0:T(8,128)}) %reduce-scatter.3.cloned.1.call-update) | async-done | bytes 524304 | tf_op jit(solution)/shard_map/reduce_scatter | solution.py:67
  228.0 1.3 copy.24
  229.3 26.1 %all_to_all.130 = f32[2,8,64,128]{3,1,0,2:T(8,128)S(1)} all-to-all(f32[2,8,64,128]{3,1,0,2:T(8,128)S(1)} %copy.24), channel_id=1, replica_groups=mesh['freq'=32,'src'=8] {'freq'}, dimensions={2} | all-to-all | bytes 1048576 | tf_op jit(solution)/shard_map/all_to_all | solution.py:27
  255.5 1.4 fusion.119
  256.9 1.4 fusion.146
  258.2 1.4 fusion.99
  259.6 1.6 fusion.141
  261.2 1.4 fusion.98
  262.6 1.6 fusion.144
  264.3 1.6 fusion.88
  265.9 1.6 fusion.89
  268.0 22.4 %all_to_all.131 = f32[2,256,2,128]{3,2,0,1:T(2,128)S(1)} all-to-all(f32[2,256,2,128]{3,2,0,1:T(2,128)S(1)} %copy.26), channel_id=1, replica_groups=mesh['freq'=32,'src'=8] {'freq'}, dimensions={1} | all-to-all | bytes 1048576 | tf_op jit(solution)/shard_map/all_to_all | solution.py:40
  292.0 56.5 %all-gather.5.cloned.1.call-done = f32[2,8,64,1024]{3,2,1,0:T(8,128)} async-done(((f32[2,8,64,128]{3,2,1,0:T(8,128)}), f32[2,8,64,1024]{3,2,1,0:T(8,128)}) %all-gather.5.cloned.1.call-update) | async-done | bytes 4194320 | tf_op jit(solution)/shard_map/all_gather | solution.py:50
  348.5 7.4 %fusion.4 = f32[8,64,128]{2,1,0:T(8,128)S(1)} fusion(f32[2,8,128,1024]{3,2,1,0:T(8,128)} %param.3, f32[2,8,64,1024]{3,2,1,0:T(8,128)} %all-gather.5.cloned.1.call-done), kind=kOutput, calls=%fused_computation.6 | convolution fusion | flops 805306368 | bytes 6553600 | tf_op jit(solution)/shard_map/idt,iqt->iqd/dot_general | solution.py:23
  355.9 7.4 %fusion.6 = f32[8,64,128]{2,1,0:T(8,128)S(1)} fusion(f32[2,8,128,1024]{3,2,1,0:T(8,128)} %param.3, f32[2,8,64,1024]{3,2,1,0:T(8,128)} %all-gather.5.cloned.1.call-done), kind=kOutput, calls=%fused_computation.8 | convolution fusion | flops 805306368 | bytes 6553600 | tf_op jit(solution)/shard_map/idt,iqt->iqd/dot_general | solution.py:23
  363.4 6.2 %fusion.77 = f32[1,8,64,128]{3,2,1,0:T(8,128)S(1)} fusion(f32[8,64,128]{2,1,0:T(8,128)S(1)} %fusion.4, f32[2,8,128,1024]{3,2,1,0:T(8,128)} %param.3, f32[2,8,64,1024]{3,2,1,0:T(8,128)S(1)} %copy-done.1), kind=kOutput, calls=%fused_computation.65 | convolution fusion | flops 805371904 | bytes 6815744 | tf_op jit(solution)/shard_map/idt,iqt->iqd/dot_general | solution.py:23
  369.6 4.4 fusion.71
  374.4 30.1 %all_to_all.132 = f32[2,8,64,128]{3,1,0,2:T(8,128)S(1)} all-to-all(f32[2,8,64,128]{3,1,0,2:T(8,128)S(1)} %copy.28), channel_id=1, replica_groups=mesh['freq'=32,'src'=8] {'freq'}, dimensions={2} | all-to-all | bytes 1048576 | tf_op jit(solution)/shard_map/all_to_all | solution.py:27
  404.6 1.4 fusion.114
  406.0 1.4 fusion.139
  407.3 1.4 fusion.101
  408.7 1.6 fusion.134
  410.3 1.4 fusion.100
  411.7 1.6 fusion.137
  413.3 1.6 fusion.84
  415.0 1.6 fusion.85
  417.1 22.7 %all_to_all.133 = f32[2,256,2,128]{3,2,0,1:T(2,128)S(1)} all-to-all(f32[2,256,2,128]{3,2,0,1:T(2,128)S(1)} %copy.30), channel_id=1, replica_groups=mesh['freq'=32,'src'=8] {'freq'}, dimensions={1} | all-to-all | bytes 1048576 | tf_op jit(solution)/shard_map/all_to_all | solution.py:40
  440.1 2.4 fusion
  442.5 2.4 fusion.2
  444.9 2.4 subtract_bitcast_fusion
  447.3 2.4 add_bitcast_fusion
  449.7 2.5 pad_maximum_fusion.1
  452.2 50.6 %reduce-scatter.5.cloned.1.call-done = f32[2,8,64,128]{3,2,1,0:T(8,128)} async-done(((f32[2,8,64,1024]{3,2,1,0:T(8,128)}), f32[2,8,64,128]{3,2,1,0:T(8,128)}) %reduce-scatter.5.cloned.1.call-update) | async-done | bytes 524304 | tf_op jit(solution)/shard_map/reduce_scatter | solution.py:67
  504.2 26.3 %all_to_all.134 = f32[2,8,64,128]{3,1,0,2:T(8,128)S(1)} all-to-all(f32[2,8,64,128]{3,1,0,2:T(8,128)S(1)} %copy.32), channel_id=1, replica_groups=mesh['freq'=32,'src'=8] {'freq'}, dimensions={2} | all-to-all | bytes 1048576 | tf_op jit(solution)/shard_map/all_to_all | solution.py:27
  530.6 1.4 fusion.109
  531.9 1.4 fusion.132
  533.3 1.4 fusion.103
  534.7 1.6 fusion.127
  536.3 1.4 fusion.102
  537.7 1.6 fusion.130
  539.3 1.6 fusion.80
  540.9 1.6 fusion.81
  543.0 22.6 %all_to_all.135 = f32[2,256,2,128]{3,2,0,1:T(2,128)S(1)} all-to-all(f32[2,256,2,128]{3,2,0,1:T(2,128)S(1)} %copy.34), channel_id=1, replica_groups=mesh['freq'=32,'src'=8] {'freq'}, dimensions={1} | all-to-all | bytes 1048576 | tf_op jit(solution)/shard_map/all_to_all | solution.py:40
  (56 shorter events, 8.9 us)
Async XLA Ops:
  7.2 67.3 %all-gather.3.cloned.1.call-start = ((), (), s32[]{:S(2)}) async-start(), calls=%async_computation.10 | async-start | bytes 4718592 | tf_op jit(solution)/shard_map/all_gather | solution.py:50
  74.4 14.8 %copy-start = (f32[2,8,128,1024]{3,2,1,0:T(8,128)S(1)}, f32[2,8,128,1024]{3,2,1,0:T(8,128)}, u32[]{:S(2)}) copy-start(f32[2,8,128,1024]{3,2,1,0:T(8,128)} %param.3) | copy-start | bytes 25165828
  81.8 7.4 %copy-start.2 = (f32[2,8,64,1024]{3,2,1,0:T(8,128)S(1)}, f32[2,8,64,1024]{3,2,1,0:T(8,128)}, u32[]{:S(2)}) copy-start(f32[2,8,64,1024]{3,2,1,0:T(8,128)} %all-gather.3.cloned.1.call-done) | copy-start | bytes 12582916
  98.6 34.1 %copy-start.5 = (s32[2,128]{1,0:T(2,128)S(1)}, s32[2,128]{1,0:T(2,128)}, u32[]{:S(2)}) copy-start(s32[2,128]{1,0:T(2,128)} %param.5) | copy-start | bytes 3076
  99.8 30.1 %all-to-all-start = ((f32[2,8,64,128]{3,1,0,2:T(8,128)}), f32[2,8,64,128]{3,1,0,2:T(8,128)S(1)}, u32[]{:S(2)}, u32[]{:S(2)}) async-start(f32[2,8,64,128]{3,1,0,2:T(8,128)} %copy.20), calls=%async_computation | async-start | bytes 1048576 | tf_op jit(solution)/shard_map/all_to_all | solution.py:27
  111.5 116.4 %reduce-scatter.3.cloned.1.call-start = ((), (), s32[]{:S(2)}) async-start(), calls=%async_computation.11 | async-start | bytes 4718592 | tf_op jit(solution)/shard_map/reduce_scatter | solution.py:67
  129.9 35.6 %slice-start = ((s8[8388608]{0:T(1024)(128)(4,1)}), s8[4194304]{0:T(1024)(128)(4,1)S(1)}, s32[]{:S(2)}) async-start(s8[8388608]{0:T(1024)(128)(4,1)} %bitcast.281), calls=%async_computation.14 | async-start | bytes 8388608
  138.7 26.8 %slice-start.1 = ((s8[8388608]{0:T(1024)(128)(4,1)}), s8[4194304]{0:T(1024)(128)(4,1)S(1)}, s32[]{:S(2)}) async-start(s8[8388608]{0:T(1024)(128)(4,1)} %bitcast.281), calls=%async_computation.15 | async-start | bytes 8388608
  177.5 171.1 %all-gather.5.cloned.1.call-start = ((), (), s32[]{:S(2)}) async-start(), calls=%async_computation.12 | async-start | bytes 4718592 | tf_op jit(solution)/shard_map/all_gather | solution.py:50
  262.6 28.0 %copy-start.3 = (f32[2,8,64,128]{3,2,1,0:T(8,128)S(1)}, f32[2,8,64,128]{3,2,1,0:T(8,128)}, u32[]{:S(2)}) copy-start(f32[2,8,64,128]{3,2,1,0:T(8,128)} %param.4) | copy-start | bytes 1572868
  291.5 211.3 %reduce-scatter.5.cloned.1.call-start = ((), (), s32[]{:S(2)}) async-start(), calls=%async_computation.13 | async-start | bytes 4718592 | tf_op jit(solution)/shard_map/reduce_scatter | solution.py:67
  348.5 14.8 %copy-start.1 = (f32[2,8,64,1024]{3,2,1,0:T(8,128)S(1)}, f32[2,8,64,1024]{3,2,1,0:T(8,128)}, u32[]{:S(2)}) copy-start(f32[2,8,64,1024]{3,2,1,0:T(8,128)} %all-gather.5.cloned.1.call-done) | copy-start | bytes 12582916
  348.5 21.1 %slice-start.2 = ((s8[8388608]{0:T(1024)(128)(4,1)}), s8[4194304]{0:T(1024)(128)(4,1)S(1)}, s32[]{:S(2)}) async-start(s8[8388608]{0:T(1024)(128)(4,1)} %bitcast.283), calls=%async_computation.16 | async-start | bytes 8388608
  355.9 13.7 %slice-start.3 = ((s8[8388608]{0:T(1024)(128)(4,1)}), s8[4194304]{0:T(1024)(128)(4,1)S(1)}, s32[]{:S(2)}) async-start(s8[8388608]{0:T(1024)(128)(4,1)} %bitcast.283), calls=%async_computation.17 | async-start | bytes 8388608
  440.0 4.9 copy-start.4
Sparse Core Ops, SparseCore 0:
  9.7 64.6 all-gather.2
  177.6 50.3 reduce-scatter.2
  291.7 56.8 all-gather.4
  452.3 50.4 reduce-scatter.4
where the time goes:
time: 583 us; the launch traced here: 574 us
  waiting for transfers between devices  243 us (42%)
  blocking collectives  173 us (30%)
  matrix products  117 us (20%)
  between operations  14.9 us (3%)
  starting transfers between devices  12.3 us (2%)
  local copies, waits for them, and re-layouts  7.05 us (1%)
  other arithmetic  6.65 us (1%)
    all_gather x2, waiting for transfers between devices, per_device(): fragment_list = lax.all_gather(downgoing, 'src', axis=3, tiled=True)  123 us
    reduce_scatter x2, waiting for transfers between devices, per_device(): lax.psum_scatter(jnp.stack([running_real_total, partial_imag]), 'src', sc...  101 us
    all_to_all x4, blocking collectives, windowed(): lax.all_to_all(jnp.stack([back_real, back_imag]), 'freq', split_axis=1, c...  90.4 us
    all_to_all x3, blocking collectives, windowed(): lax.all_to_all(spectra, 'freq', split_axis=2, concat_axis=1, tiled=True)  82.6 us
    dot_general x16, matrix products, product(): return jnp.einsum(layout_kind, left, right, precision=lax.Precision.HIGHEST)  68.8 us
    dot_general x32, matrix products, transform(): jnp.einsum('tf,fpx->tpx', table, sample_values, precision=lax.Precision.H...  47.7 us
    all_to_all x1, waiting for transfers between devices, windowed(): lax.all_to_all(spectra, 'freq', split_axis=2, concat_axis=1, tiled=True)  18.3 us
    all_to_all x1, starting transfers between devices, windowed(): lax.all_to_all(spectra, 'freq', split_axis=2, concat_axis=1, tiled=True)  11.8 us
  transfers between devices with their start and end apart: 5, of which 5 were waited for; matrix products, arithmetic and copies ran while one was open for 0% of the time, Pallas kernels for 0%

commit v1 on v0

v1 whole, which is shorter than its diff:
```python
import math

import jax
import jax.numpy as jnp
import ml_dtypes
import numpy as np
from jax import lax
from jax.experimental import pallas as pl
from jax.experimental.pallas import tpu as pltpu
from jax.sharding import PartitionSpec as P

ITERS = 2
NFD = 32
NSD = 8
NY = 4
FL = 8
NC = 2
NQ = 32
MSG = 2 * FL
ROWS = NQ * MSG
HALF = ROWS // 2
LANES = 128
NF = 256
MESH = pl.DeviceIdType.MESH
F32 = jnp.float32
BF16 = jnp.bfloat16


def tables():
    samples = np.arange(NF)
    angles = (samples[:, None] * samples[None, :] % NF) * (2.0 * math.pi / NF)
    table = np.concatenate([np.cos(angles), np.sin(angles)], 0).astype(np.float32)
    high = table.astype(ml_dtypes.bfloat16)
    low = (table - high.astype(np.float32)).astype(ml_dtypes.bfloat16)
    return high, low


def split(values):
    high = values.astype(BF16)
    return high, (values - high.astype(F32)).astype(BF16)


def dot(left, right):
    return jnp.dot(left, right, preferred_element_type=F32)


def dot_t(left, right):
    return lax.dot_general(left, right, (((1,), (1,)), ((), ())), preferred_element_type=F32)


def kernel(
    refl, foc, onsets, th, tl, down_out, up_out,
    rstage, rhi, rlo, ag, part, r1, r2, rz, sbuf, rbuf,
    stage_sem, a2a_send, a2a_recv, ag_send, ag_recv, rs_send, rs_recv,
):
    me = lax.axis_index("freq")
    src = lax.axis_index("src")
    z = src // NY
    y = lax.rem(src, NY)
    z1 = 1 - z
    yp = lax.rem(y + 1, NY)
    ym = lax.rem(y + NY - 1, NY)
    y2 = lax.rem(y + 2, NY)
    dev_p = (me, z * NY + yp)
    dev_m = (me, z * NY + ym)
    dev_z = (me, z1 * NY + y)
    pending = []

    barrier = pltpu.get_barrier_semaphore()
    for dev in (dev_p, dev_m, dev_z):
        pl.semaphore_signal(barrier, inc=1, device_id=dev, device_id_type=MESH)

    def greet(k, carry):
        pl.semaphore_signal(
            barrier, inc=1, device_id=(lax.rem(me + k, NFD), src), device_id_type=MESH
        )
        return carry

    lax.fori_loop(1, NFD, greet, 0)

    def stage_copy(f):
        return pltpu.make_async_copy(refl.at[:, f], rstage.at[f % 2], stage_sem.at[f % 2])

    stage_copy(0).start()
    stage_copy(1).start()

    def lay_out(h):
        for c in range(2):
            for f in range(FL):
                ag[0, h, src, pl.ds(c * FL + f, NQ, stride=MSG), :] = foc[
                    c, f, pl.ds(h, NQ, stride=NC), :
                ]

    def prepare(f):
        stage_copy(f).wait()
        for c in range(2):
            high, low = split(rstage[f % 2, c])
            rhi[f, c * LANES : (c + 1) * LANES, :] = high
            rlo[f, c * LANES : (c + 1) * LANES, :] = low
        if f + 2 < FL:
            stage_copy(f + 2).start()

    def rows_of(half):
        return pl.ds(half * HALF, HALF)

    def remote(source, target, send_sem, recv_sem, dev):
        copy = pltpu.make_async_remote_copy(
            source, target, send_sem, recv_sem, device_id=dev, device_id_type=MESH
        )
        copy.start()
        pending.append(copy)

    def landed(target, sem):
        pltpu.make_async_copy(target, target, sem).wait()

    def ag_msg(it, h, slot, half, number, dev):
        piece = ag.at[it, h, slot, rows_of(half)]
        remote(piece, piece, ag_send.at[it, h, number], ag_recv.at[it, h, number], dev)

    def ag_landed(it, h, slot, half, number):
        landed(ag.at[it, h, slot, rows_of(half)], ag_recv.at[it, h, number])

    def ag_start(it, h):
        for half in range(2):
            ag_msg(it, h, src, half, half, dev_z)
            ag_msg(it, h, src, half, 2 + half, dev_p)
            ag_msg(it, h, src, 1 - half, 4 + 1 - half, dev_m)

    def ag_forward_z(it, h):
        other = z1 * NY + y
        for half in range(2):
            ag_landed(it, h, other, half, half)
            ag_msg(it, h, other, half, 6 + half, dev_p)
            ag_msg(it, h, other, half, 8 + half, dev_m)

    def ag_forward_y(it, h):
        for row, base, number in ((z, 2, 10), (z1, 6, 12)):
            ag_landed(it, h, row * NY + ym, 0, base)
            ag_msg(it, h, row * NY + ym, 0, number, dev_p)
            ag_landed(it, h, row * NY + yp, 1, base + 3)
            ag_msg(it, h, row * NY + yp, 1, number + 1, dev_m)

    def ag_finish(it, h):
        for row, base, number in ((z, 2, 10), (z1, 6, 12)):
            ag_landed(it, h, row * NY + ym, 1, base + 1)
            ag_landed(it, h, row * NY + yp, 0, base + 2)
            ag_landed(it, h, row * NY + y2, 0, number)
            ag_landed(it, h, row * NY + y2, 1, number + 1)

    def a2a_start(it, h, k):
        def send(step, carry):
            peer = lax.rem(me + step, NFD)
            pltpu.make_async_remote_copy(
                sbuf.at[it, h, k, pl.ds(pl.multiple_of(peer * MSG, MSG), MSG)],
                rbuf.at[it, h, k, pl.ds(pl.multiple_of(me * MSG, MSG), MSG)],
                a2a_send.at[it, h, k],
                a2a_recv.at[it, h, k],
                device_id=(peer, src),
                device_id_type=MESH,
            ).start()
            return carry

        lax.fori_loop(1, NFD, send, 0)
        own = pl.ds(pl.multiple_of(me * MSG, MSG), MSG)
        rbuf[it, h, k, own, :] = sbuf[it, h, k, own, :]

    def a2a_wait(it, h, k):
        landed(rbuf.at[it, h, k, pl.ds(0, ROWS - MSG)], a2a_recv.at[it, h, k])

    def a2a_sent(it, h, k):
        landed(sbuf.at[it, h, k, pl.ds(0, ROWS - MSG)], a2a_send.at[it, h, k])

    def forward(it, h):
        def one(f, carry):
            real = [ag[it, h, s, pl.ds(f, NQ, stride=MSG), :] for s in range(NSD)]
            imag = [ag[it, h, s, pl.ds(FL + f, NQ, stride=MSG), :] for s in range(NSD)]
            field = jnp.concatenate(
                [jnp.concatenate(real, axis=1), jnp.concatenate(imag, axis=1)], axis=0
            )
            high, low = split(field)
            both = dot_t(jnp.concatenate([high, low], axis=0), rhi[f])
            total = both[: 2 * NQ] + both[2 * NQ :] + dot_t(high, rlo[f])
            sbuf[it, h, 0, pl.ds(f, NQ, stride=MSG), :] = (
                total[:NQ, :LANES] - total[NQ:, LANES:]
            )
            sbuf[it, h, 0, pl.ds(FL + f, NQ, stride=MSG), :] = (
                total[:NQ, LANES:] + total[NQ:, :LANES]
            )
            return carry

        lax.fori_loop(0, FL, one, 0)
        a2a_start(it, h, 0)

    def transform(values):
        high, low = split(values)
        return dot(th[...], high) + (dot(tl[...], high) + dot(th[...], low))

    def window(it, h, k):
        a2a_wait(it, h, k)
        received = rbuf[it, h, k].reshape(NFD, 2, FL, LANES)
        spectra = jnp.concatenate(
            [received[:, 0].reshape(NF, LANES), received[:, 1].reshape(NF, LANES)], axis=1
        )
        times = transform(spectra)
        sample = lax.broadcasted_iota(jnp.int32, (NF, LANES), 0)
        nearest = jnp.minimum(sample, NF - sample)
        kept = jnp.where(nearest < onsets[h : h + 1, :], 1.0 / NF, 0.0).astype(F32)
        real = (times[:NF, :LANES] - times[NF:, LANES:]) * kept
        imag = (times[NF:, :LANES] + times[:NF, LANES:]) * kept
        back = transform(jnp.concatenate([real, imag], axis=1))
        back_real = back[:NF, :LANES] + back[NF:, LANES:]
        back_imag = back[:NF, LANES:] - back[NF:, :LANES]
        sbuf[it, h, k + 1] = jnp.concatenate(
            [back_real.reshape(NFD, 1, FL, LANES), back_imag.reshape(NFD, 1, FL, LANES)], axis=1
        ).reshape(ROWS, LANES)
        a2a_start(it, h, k + 1)

    def rs_msg(source, target, it, h, number, dev):
        remote(source, target, rs_send.at[it, h, number], rs_recv.at[it, h, number], dev)

    def rs_second(it, h, row, direction, half):
        column, dev = ((yp, dev_p), (ym, dev_m))[direction]
        rs_msg(
            part.at[it, h, row * NY + column, rows_of(half)],
            r2.at[it, h, row * 2 + direction, rows_of(half)],
            it, h, 4 + row * 4 + direction * 2 + half, dev,
        )

    def adjoint(it, h):
        a2a_wait(it, h, 1)

        def one(f, carry):
            real = rbuf[it, h, 1, pl.ds(f, NQ, stride=MSG), :]
            imag = rbuf[it, h, 1, pl.ds(FL + f, NQ, stride=MSG), :]
            field = jnp.concatenate(
                [
                    jnp.concatenate([real, imag], axis=1),
                    jnp.concatenate([imag, -real], axis=1),
                ],
                axis=0,
            )
            high, low = split(field)
            both = dot(jnp.concatenate([high, low], axis=0), rhi[f])
            total = both[: 2 * NQ] + both[2 * NQ :] + dot(high, rlo[f])
            for s in range(NSD):
                columns = slice(s * LANES, (s + 1) * LANES)
                part[it, h, s, pl.ds(f, NQ, stride=MSG), :] = total[:NQ, columns]
                part[it, h, s, pl.ds(FL + f, NQ, stride=MSG), :] = total[NQ:, columns]
            return carry

        lax.fori_loop(0, FL, one, 0)
        for row in range(2):
            for half, dev in ((0, dev_p), (1, dev_m)):
                rs_msg(
                    part.at[it, h, row * NY + y2, rows_of(half)],
                    r1.at[it, h, row * 2 + half],
                    it, h, row * 2 + half, dev,
                )
        for row in range(2):
            rs_second(it, h, row, 0, 1)
            rs_second(it, h, row, 1, 0)

    def rs_middle(it, h):
        for row in range(2):
            for half, column in ((0, yp), (1, ym)):
                landed(r1.at[it, h, row * 2 + half], rs_recv.at[it, h, row * 2 + half])
                slot = row * NY + column
                part[it, h, slot, rows_of(half), :] += r1[it, h, row * 2 + half]
                rs_second(it, h, row, half, half)

    def rs_column(it, h, row, half):
        for direction in range(2):
            landed(
                r2.at[it, h, row * 2 + direction, rows_of(half)],
                rs_recv.at[it, h, 4 + row * 4 + direction * 2 + half],
            )
        slot = row * NY + y
        part[it, h, slot, rows_of(half), :] += (
            r2[it, h, row * 2, rows_of(half), :] + r2[it, h, row * 2 + 1, rows_of(half), :]
        )

    def rs_columns(it, h):
        for half in range(2):
            rs_column(it, h, z1, half)
            rs_msg(
                part.at[it, h, z1 * NY + y, rows_of(half)],
                rz.at[it, h, rows_of(half)],
                it, h, 12 + half, dev_z,
            )
        for half in range(2):
            rs_column(it, h, z, half)

    def rs_finish(it, h):
        for half in range(2):
            landed(rz.at[it, h, rows_of(half)], rs_recv.at[it, h, 12 + half])
            sbuf[it, h, 2, rows_of(half), :] = (
                part[it, h, src, rows_of(half), :] + rz[it, h, rows_of(half), :]
            )
        a2a_start(it, h, 2)

    def update(it, h):
        a2a_wait(it, h, 3)
        if it + 1 < ITERS:
            ag[it + 1, h, src] = ag[0, h, src] - rbuf[it, h, 3]
            ag_start(it + 1, h)
        else:
            for c in range(2):
                for f in range(FL):
                    rows = pl.ds(c * FL + f, NQ, stride=MSG)
                    down_out[c, f, pl.ds(h, NQ, stride=NC), :] = (
                        ag[0, h, src, rows, :] - rbuf[it, h, 3, rows, :]
                    )

    def write_upgoing(h):
        for c in range(2):
            for f in range(FL):
                up_out[c, f, pl.ds(h, NQ, stride=NC), :] = rbuf[
                    ITERS - 1, h, 1, pl.ds(c * FL + f, NQ, stride=MSG), :
                ]

    lay_out(0)
    pl.semaphore_wait(barrier, NFD - 1 + 3)
    ag_start(0, 0)
    lay_out(1)
    for f in range(3):
        prepare(f)
    ag_forward_z(0, 0)
    for f in range(3, 6):
        prepare(f)
    ag_forward_y(0, 0)
    for f in range(6, FL):
        prepare(f)
    ag_start(0, 1)
    ag_finish(0, 0)
    for it in range(ITERS):
        forward(it, 0)
        if it:
            update(it - 1, 1)
        ag_forward_z(it, 1)
        ag_forward_y(it, 1)
        window(it, 0, 0)
        ag_finish(it, 1)
        forward(it, 1)
        adjoint(it, 0)
        window(it, 1, 0)
        rs_middle(it, 0)
        rs_columns(it, 0)
        adjoint(it, 1)
        rs_finish(it, 0)
        if it == ITERS - 1:
            write_upgoing(0)
        rs_middle(it, 1)
        window(it, 0, 2)
        rs_columns(it, 1)
        update(it, 0)
        rs_finish(it, 1)
        if it + 1 < ITERS:
            ag_forward_z(it + 1, 0)
            ag_forward_y(it + 1, 0)
            window(it, 1, 2)
            ag_finish(it + 1, 0)
        else:
            write_upgoing(1)
            window(it, 1, 2)
            update(it, 1)

    for copy in pending:
        copy.wait_send()
    for it in range(ITERS):
        for h in range(NC):
            for k in range(4):
                a2a_sent(it, h, k)


def per_device(reflection, focusing, onsets):
    high, low = tables()
    vmem = pl.BlockSpec(memory_space=pltpu.VMEM)
    block = jax.ShapeDtypeStruct(focusing.shape, F32)
    return pl.pallas_call(
        kernel,
        out_shape=(block, block),
        in_specs=[pl.BlockSpec(memory_space=pl.ANY), vmem, vmem, vmem, vmem],
        out_specs=(vmem, vmem),
        scratch_shapes=[
            pltpu.VMEM((2, 2, LANES, 1024), F32),
            pltpu.VMEM((FL, 2 * LANES, 1024), BF16),
            pltpu.VMEM((FL, 2 * LANES, 1024), BF16),
            pltpu.VMEM((ITERS, NC, NSD, ROWS, LANES), F32),
            pltpu.VMEM((ITERS, NC, NSD, ROWS, LANES), F32),
            pltpu.VMEM((ITERS, NC, 4, HALF, LANES), F32),
            pltpu.VMEM((ITERS, NC, 4, ROWS, LANES), F32),
            pltpu.VMEM((ITERS, NC, ROWS, LANES), F32),
            pltpu.VMEM((ITERS, NC, 4, ROWS, LANES), F32),
            pltpu.VMEM((ITERS, NC, 4, ROWS, LANES), F32),
            pltpu.SemaphoreType.DMA((2,)),
            pltpu.SemaphoreType.DMA((ITERS, NC, 4)),
            pltpu.SemaphoreType.DMA((ITERS, NC, 4)),
            pltpu.SemaphoreType.DMA((ITERS, NC, 14)),
            pltpu.SemaphoreType.DMA((ITERS, NC, 14)),
            pltpu.SemaphoreType.DMA((ITERS, NC, 14)),
            pltpu.SemaphoreType.DMA((ITERS, NC, 14)),
        ],
        compiler_params=pltpu.CompilerParams(
            collective_id=0, has_side_effects=True, vmem_limit_bytes=56 * 1024 * 1024
        ),
        name="marchenko",
    )(reflection, focusing, onsets, jnp.asarray(high), jnp.asarray(low))


def solution(mesh):
    placed = (P(None, "freq", "src", None), P(None, "freq", None, "src"), P("freq", "src"))
    return jax.shard_map(
        per_device,
        mesh=mesh,
        in_specs=placed,
        out_specs=(P(None, "freq", None, "src"), P(None, "freq", None, "src")),
        check_vma=False,
    )
```

time: 583 us -> 240 us (0.41); the launches traced: 574 us -> 239 us
  waiting for transfers between devices: 243 us -> 0 us
  Pallas kernels: 0 us -> 235 us
  blocking collectives: 173 us -> 0 us
  matrix products: 117 us -> 0 us
  between operations: 14.9 us -> 0.64 us
  starting transfers between devices: 12.3 us -> 0 us
  other arithmetic: 6.65 us -> 0 us
    pallas_call x0 -> x1, Pallas kernels: none -> 235 us  [per_device(): pl.pallas_call(kernel, out_shape=(block, block), in_specs=[pl.BlockSpec(m...]
    all_to_all x7 -> x0, blocking collectives: 173 us -> none  [the longest x4 90.4 us: windowed(): lax.all_to_all(jnp.stack([back_real, back_imag]), 'freq', split_axis=1, c...]
    all_gather x2 -> x0, waiting for transfers between devices: 123 us -> none  [per_device(): fragment_list = lax.all_gather(downgoing, 'src', axis=3, tiled=True)]
    dot_general x48 -> x0, matrix products: 117 us -> none  [the longest x16 68.8 us: product(): return jnp.einsum(layout_kind, left, right, precision=lax.Precision.HIGHEST)]
    reduce_scatter x2 -> x0, waiting for transfers between devices: 101 us -> none  [per_device(): lax.psum_scatter(jnp.stack([running_real_total, partial_imag]), 'src', sc...]
    all_to_all x1 -> x0, waiting for transfers between devices: 18.3 us -> none  [windowed(): lax.all_to_all(spectra, 'freq', split_axis=2, concat_axis=1, tiled=True)]
    all_to_all x1 -> x0, starting transfers between devices: 11.8 us -> none  [windowed(): lax.all_to_all(spectra, 'freq', split_axis=2, concat_axis=1, tiled=True)]
  transfers between devices with their start and end apart: 5 -> 0, of which waited for: 5 -> 0; matrix products, arithmetic and copies ran while one was open for 0% -> 0% of each run, Pallas kernels for 0% -> 0%
where the time goes in v1:
time: 240 us; the launch traced here: 239 us
  Pallas kernels  235 us (98%)
  local copies, waits for them, and re-layouts  3.77 us (2%)
    pallas_call x1, Pallas kernels, per_device(): pl.pallas_call(kernel, out_shape=(block, block), in_specs=[pl.BlockSpec(m...  235 us

profile of v1, /device:TPU:1, one launch (start us, length us, event | category | flops | bytes accessed | tf_op | source)
XLA Modules:
  0.0 239.5 jit_solution(10214968878072181029)
XLA Ops:
  0.6 235.1 %marchenko.1 = (f32[2,8,64,128]{3,2,1,0:T(8,128)}, f32[2,8,64,128]{3,2,1,0:T(8,128)}) custom-call(f32[2,8,128,1024]{3,2,1,0:T(8,128)} %refl.1, f32[2,8,64,128]{3,2,1,0:T(8,128)} %foc.1, s32[2,128]{1,0:T(2,128)} %onsets.1, bf16[512,256]{1,0:T(8,128)(2,1)} %constant.4.clone.th, bf16[512,256]{1,0:T(8,128)(2,1)} %constant.5.clone.tl), custom_call_target="tpu_custom_call" | custom-call | tf_op jit(solution)/shard_map/marchenko/pallas_call | solution.py:379
  235.7 1.9 copy.9
  237.6 1.9 copy.10

commit v2 on v1

v2 whole, which is shorter than its diff:
```python
import math

import jax
import jax.numpy as jnp
import ml_dtypes
import numpy as np
from jax import lax
from jax.experimental import pallas as pl
from jax.experimental.pallas import tpu as pltpu
from jax.sharding import PartitionSpec as P

ITERS = 2
NFD = 32
NSD = 8
NY = 4
FL = 8
NP = 64
NC = 4
NQ = NP // NC
NW = NC // 2
MSG = 2 * FL
ROWS = NQ * MSG
FROWS = 2 * NQ
HALF = ROWS // 2
TRACES = NFD * MSG
LANES = 128
NF = 256
ORDER = (
    "ags 0 0", "ags 0 1", "prep", "prep", "prep", "prep", "agz 0 0", "prep", "prep", "agz 0 1",
    "prep", "prep", "agy 0 0", "ags 0 2", "ags 0 3", "agy 0 1", "agz 0 2", "agf 0 0", "fwd 0 0",
    "agz 0 3", "win 0 0", "agf 0 1", "fwd 0 1", "agy 0 2", "agy 0 3", "adj 0 0", "win 0 1",
    "agf 0 2", "fwd 0 2", "rsm 0 0", "agf 0 3", "fwd 0 3", "adj 0 1", "rsc 0 0", "win 0 2",
    "win 0 3", "rsm 0 1", "rsf 0 0", "adj 0 2", "rsc 0 1", "adj 0 3", "win2 0 0", "rsm 0 2",
    "rsf 0 1", "rsm 0 3", "upd 0 0", "agz 1 0", "win2 0 1", "rsc 0 2", "rsc 0 3", "upd 0 1",
    "agz 1 1", "agy 1 0", "rsf 0 2", "rsf 0 3", "agy 1 1", "win2 0 2", "agf 1 0", "fwd 1 0",
    "win2 0 3", "agf 1 1", "fwd 1 1", "upd 0 2", "agz 1 2", "win 1 0", "upd 0 3", "agz 1 3",
    "agy 1 2", "win 1 1", "agy 1 3", "adj 1 0", "agf 1 2", "fwd 1 2", "agf 1 3", "fwd 1 3",
    "rsm 1 0", "adj 1 1", "win 1 2", "rsc 1 0", "win 1 3", "rsm 1 1", "adj 1 2", "rsf 1 0",
    "rsc 1 1", "adj 1 3", "win2 1 0", "rsm 1 2", "rsf 1 1", "rsm 1 3", "upd 1 0", "rsc 1 2",
    "win2 1 1", "rsc 1 3", "rsf 1 2", "upd 1 1", "rsf 1 3", "win2 1 2", "win2 1 3", "upd 1 2",
    "upd 1 3",
)
MESH = pl.DeviceIdType.MESH
F32 = jnp.float32
BF16 = jnp.bfloat16


def tables():
    samples = np.arange(NF)
    angles = (samples[:, None] * samples[None, :] % NF) * (2.0 * math.pi / NF)
    table = np.concatenate([np.cos(angles), np.sin(angles)], 0).astype(np.float32)
    high = table.astype(ml_dtypes.bfloat16)
    low = (table - high.astype(np.float32)).astype(ml_dtypes.bfloat16)
    return high, low


def split(values):
    high = values.astype(BF16)
    return high, (values - high.astype(F32)).astype(BF16)


def dot(left, right):
    return jnp.dot(left, right, preferred_element_type=F32)


def kernel(
    refl, foc, onsets, th, tl, down_out, up_out,
    rstage, rhi, rlo, thi, tlo, ag, part, r1, r2, rz, sfield, rfield, straces, rtraces,
    stage_sem, a2a_send, a2a_recv, ag_send, ag_recv, rs_send, rs_recv, entered,
):
    me = lax.axis_index("freq")
    src = lax.axis_index("src")
    z = src // NY
    y = lax.rem(src, NY)
    z1 = 1 - z
    yp = lax.rem(y + 1, NY)
    ym = lax.rem(y + NY - 1, NY)
    y2 = lax.rem(y + 2, NY)
    dev_p = (me, z * NY + yp)
    dev_m = (me, z * NY + ym)
    dev_z = (me, z1 * NY + y)

    z_hi, x, core = me // 8, lax.rem(me // 2, 4), lax.rem(me, 2)
    along_x = [(z_hi * 8 + lax.rem(x + k, 4) * 2 + core, src) for k in (1, 2, 3)]
    along_z = [(lax.rem(z_hi + k, 4) * 8 + x * 2 + core, src) for k in (1, 2, 3)]
    sibling = (z_hi * 8 + x * 2 + 1 - core, src)
    barrier = pltpu.get_barrier_semaphore()
    greeted = [dev_p, dev_m, dev_z, sibling, *along_x, *along_z]
    for dev in greeted:
        pl.semaphore_signal(barrier, inc=1, device_id=dev, device_id_type=MESH)

    def signal_round(number, devices):
        for dev in devices:
            pl.semaphore_signal(entered.at[number], inc=1, device_id=dev, device_id_type=MESH)

    def stage_copy(f):
        return pltpu.make_async_copy(refl.at[:, f], rstage.at[f % 2], stage_sem.at[f % 2])

    stage_copy(0).start()
    stage_copy(1).start()

    def lay_out(h):
        for c in range(2):
            for f in range(FL):
                ag[0, h, src, f * FROWS + c * NQ : f * FROWS + (c + 1) * NQ, :] = foc[
                    c, f, pl.ds(h, NQ, stride=NC), :
                ]

    def prepare(f):
        stage_copy(f).wait()
        for c in range(2):
            high, low = split(rstage[f % 2, c])
            rows = slice(c * LANES, (c + 1) * LANES)
            rhi[f, rows, :] = high
            rlo[f, rows, :] = low
            thi[f, :, rows] = high.T
            tlo[f, :, rows] = low.T
        if f + 2 < FL:
            stage_copy(f + 2).start()

    def rows_of(half):
        return pl.ds(half * HALF, HALF)

    def remote(source, target, send_sem, recv_sem, dev):
        copy = pltpu.make_async_remote_copy(
            source, target, send_sem, recv_sem, device_id=dev, device_id_type=MESH
        )
        copy.start()

    def landed(target, sem):
        pltpu.make_async_copy(target, target, sem).wait()

    def ag_msg(it, h, slot, half, number, dev):
        piece = ag.at[it, h, slot, rows_of(half)]
        remote(piece, piece, ag_send.at[it, h], ag_recv.at[it, h, number], dev)

    def ag_landed(it, h, slot, half, number):
        landed(ag.at[it, h, slot, rows_of(half)], ag_recv.at[it, h, number])

    def ag_start(it, h):
        for half in range(2):
            ag_msg(it, h, src, half, half, dev_z)
            ag_msg(it, h, src, half, 2 + half, dev_p)
            ag_msg(it, h, src, 1 - half, 4 + 1 - half, dev_m)

    def ag_forward_z(it, h):
        other = z1 * NY + y
        for half in range(2):
            ag_landed(it, h, other, half, half)
            ag_msg(it, h, other, half, 6 + half, dev_p)
            ag_msg(it, h, other, half, 8 + half, dev_m)

    def ag_forward_y(it, h):
        for row, base, number in ((z, 2, 10), (z1, 6, 12)):
            ag_landed(it, h, row * NY + ym, 0, base)
            ag_msg(it, h, row * NY + ym, 0, number, dev_p)
            ag_landed(it, h, row * NY + yp, 1, base + 3)
            ag_msg(it, h, row * NY + yp, 1, number + 1, dev_m)

    def ag_finish(it, h):
        for row, base, number in ((z, 2, 10), (z1, 6, 12)):
            ag_landed(it, h, row * NY + ym, 1, base + 1)
            ag_landed(it, h, row * NY + yp, 0, base + 2)
            ag_landed(it, h, row * NY + y2, 0, number)
            ag_landed(it, h, row * NY + y2, 1, number + 1)

    mine = me // NW
    lane = lax.rem(me, NW)
    own_field = pl.ds(pl.multiple_of(mine * MSG, MSG), MSG)
    own_traces = pl.ds(pl.multiple_of(me * MSG, MSG), MSG)

    def a2a_copy(source, target, it, h, k, peer):
        return pltpu.make_async_remote_copy(
            source, target, a2a_send.at[it, h, k], a2a_recv.at[it, h, k],
            device_id=(peer, src), device_id_type=MESH,
        )

    def to_windows(it, h, k):
        here = h // 2

        def send(step, carry):
            q = lax.rem(mine + step, NQ)
            a2a_copy(
                sfield.at[it, h, k // 2, pl.ds(pl.multiple_of(q * MSG, MSG), MSG)],
                rtraces.at[it, h, k // 2, own_traces],
                it, h, k, q * NW + here,
            ).start()
            return carry

        lax.fori_loop(1, NQ, send, 0)

        @pl.when(lane == here)
        def _():
            rtraces[it, h, k // 2, own_traces, :] = sfield[it, h, k // 2, own_field, :]

        if NW > 1:

            @pl.when(lane != here)
            def _():
                a2a_copy(
                    sfield.at[it, h, k // 2, own_field],
                    rtraces.at[it, h, k // 2, own_traces],
                    it, h, k, mine * NW + here,
                ).start()

    def from_windows(it, h, k):
        def send(step, carry):
            peer = lax.rem(me + step, NFD)
            a2a_copy(
                straces.at[it, h, k // 2, pl.ds(pl.multiple_of(peer * MSG, MSG), MSG)],
                rfield.at[it, h, k // 2, own_field],
                it, h, k, peer,
            ).start()
            return carry

        lax.fori_loop(1, NFD, send, 0)
        rfield[it, h, k // 2, own_field, :] = straces[it, h, k // 2, own_traces, :]

    def field_wait(buffer, it, h, k, sem):
        if NW > 1:

            @pl.when(lane != h // 2)
            def _():
                landed(buffer.at[it, h, k // 2], sem.at[it, h, k])

        @pl.when(lane == h // 2)
        def _():
            landed(buffer.at[it, h, k // 2, pl.ds(0, ROWS - MSG)], sem.at[it, h, k])

    def traces_wait(buffer, it, h, k, sem):
        landed(buffer.at[it, h, k // 2, pl.ds(0, TRACES - MSG)], sem.at[it, h, k])

    def forward(it, h):
        def one(f, carry):
            rows = pl.ds(pl.multiple_of(f * FROWS, FROWS), FROWS)
            field = jnp.concatenate([ag[it, h, s, rows, :] for s in range(NSD)], axis=1)
            high, low = split(field)
            both = dot(jnp.concatenate([high, low], axis=0), thi[f])
            total = both[: 2 * NQ] + both[2 * NQ :] + dot(high, tlo[f])
            sfield[it, h, 0, pl.ds(f, NQ, stride=MSG), :] = (
                total[:NQ, :LANES] - total[NQ:, LANES:]
            )
            sfield[it, h, 0, pl.ds(FL + f, NQ, stride=MSG), :] = (
                total[:NQ, LANES:] + total[NQ:, :LANES]
            )
            return carry

        lax.fori_loop(0, FL, one, 0, unroll=2)
        to_windows(it, h, 0)

    def transform(values):
        high, low = split(values)
        return dot(th[...], high) + (dot(tl[...], high) + dot(th[...], low))

    def window(it, h, k):
        traces_wait(rtraces, it, h, k, a2a_recv)
        received = rtraces[it, h, k // 2].reshape(NFD, 2, FL, LANES)
        spectra = jnp.concatenate(
            [received[:, 0].reshape(NF, LANES), received[:, 1].reshape(NF, LANES)], axis=1
        )
        times = transform(spectra)
        sample = lax.broadcasted_iota(jnp.int32, (NF, LANES), 0)
        nearest = jnp.minimum(sample, NF - sample)
        row = h % 2
        kept = jnp.where(nearest < onsets[row : row + 1, :], 1.0 / NF, 0.0).astype(F32)
        real = (times[:NF, :LANES] - times[NF:, LANES:]) * kept
        imag = (times[NF:, :LANES] + times[:NF, LANES:]) * kept
        back = transform(jnp.concatenate([real, imag], axis=1))
        back_real = back[:NF, :LANES] + back[NF:, LANES:]
        back_imag = back[:NF, LANES:] - back[NF:, :LANES]
        straces[it, h, k // 2] = jnp.concatenate(
            [back_real.reshape(NFD, 1, FL, LANES), back_imag.reshape(NFD, 1, FL, LANES)], axis=1
        ).reshape(TRACES, LANES)
        from_windows(it, h, k + 1)

    def windowed(it, h, k):
        if NW == 1:
            window(it, h, k)
        else:
            pl.when(lane == h // 2)(lambda: window(it, h, k))

    def rs_msg(source, target, it, h, number, dev):
        remote(source, target, rs_send.at[it, h], rs_recv.at[it, h, number], dev)

    def rs_second(it, h, row, direction, half):
        column, dev = ((yp, dev_p), (ym, dev_m))[direction]
        rs_msg(
            part.at[it, h, row * NY + column, rows_of(half)],
            r2.at[it, h, row * 2 + direction, rows_of(half)],
            it, h, 4 + row * 4 + direction * 2 + half, dev,
        )

    def adjoint(it, h):
        field_wait(rfield, it, h, 1, a2a_recv)

        def one(f, carry):
            real = rfield[it, h, 0, pl.ds(f, NQ, stride=MSG), :]
            imag = rfield[it, h, 0, pl.ds(FL + f, NQ, stride=MSG), :]
            field = jnp.concatenate(
                [
                    jnp.concatenate([real, imag], axis=1),
                    jnp.concatenate([imag, -real], axis=1),
                ],
                axis=0,
            )
            high, low = split(field)
            both = dot(jnp.concatenate([high, low], axis=0), rhi[f])
            total = both[: 2 * NQ] + both[2 * NQ :] + dot(high, rlo[f])
            rows = pl.ds(pl.multiple_of(f * FROWS, FROWS), FROWS)
            for s in range(NSD):
                part[it, h, s, rows, :] = total[:, s * LANES : (s + 1) * LANES]
            return carry

        lax.fori_loop(0, FL, one, 0, unroll=2)
        if it == ITERS - 1:
            write_upgoing(h)
        for row in range(2):
            for half, dev in ((0, dev_p), (1, dev_m)):
                rs_msg(
                    part.at[it, h, row * NY + y2, rows_of(half)],
                    r1.at[it, h, row * 2 + half],
                    it, h, row * 2 + half, dev,
                )
        for row in range(2):
            rs_second(it, h, row, 0, 1)
            rs_second(it, h, row, 1, 0)

    def rs_middle(it, h):
        for row in range(2):
            for half, column in ((0, yp), (1, ym)):
                landed(r1.at[it, h, row * 2 + half], rs_recv.at[it, h, row * 2 + half])
                slot = row * NY + column
                part[it, h, slot, rows_of(half), :] += r1[it, h, row * 2 + half]
                rs_second(it, h, row, half, half)

    def rs_column(it, h, row, half):
        for direction in range(2):
            landed(
                r2.at[it, h, row * 2 + direction, rows_of(half)],
                rs_recv.at[it, h, 4 + row * 4 + direction * 2 + half],
            )
        slot = row * NY + y
        part[it, h, slot, rows_of(half), :] += (
            r2[it, h, row * 2, rows_of(half), :] + r2[it, h, row * 2 + 1, rows_of(half), :]
        )

    def rs_columns(it, h):
        for half in range(2):
            rs_column(it, h, z1, half)
            rs_msg(
                part.at[it, h, z1 * NY + y, rows_of(half)],
                rz.at[it, h, rows_of(half)],
                it, h, 12 + half, dev_z,
            )
        for half in range(2):
            rs_column(it, h, z, half)

    def rs_finish(it, h):
        for half in range(2):
            landed(rz.at[it, h, rows_of(half)], rs_recv.at[it, h, 12 + half])
            for f in range(half * FL // 2, (half + 1) * FL // 2):
                for c in range(2):
                    rows = slice(f * FROWS + c * NQ, f * FROWS + (c + 1) * NQ)
                    sfield[it, h, 1, pl.ds(c * FL + f, NQ, stride=MSG), :] = (
                        part[it, h, src, rows, :] + rz[it, h, rows, :]
                    )
        to_windows(it, h, 2)

    def update(it, h):
        field_wait(rfield, it, h, 3, a2a_recv)
        for c in range(2):
            for f in range(FL):
                rows = slice(f * FROWS + c * NQ, f * FROWS + (c + 1) * NQ)
                field = (
                    ag[0, h, src, rows, :]
                    - rfield[it, h, 1, pl.ds(c * FL + f, NQ, stride=MSG), :]
                )
                if it + 1 < ITERS:
                    ag[it + 1, h, src, rows, :] = field
                else:
                    down_out[c, f, pl.ds(h, NQ, stride=NC), :] = field
        if it + 1 < ITERS:
            ag_start(it + 1, h)

    def write_upgoing(h):
        for c in range(2):
            for f in range(FL):
                up_out[c, f, pl.ds(h, NQ, stride=NC), :] = rfield[
                    ITERS - 1, h, 0, pl.ds(c * FL + f, NQ, stride=MSG), :
                ]

    steps = {
        "agz": ag_forward_z,
        "agy": ag_forward_y,
        "agf": ag_finish,
        "fwd": forward,
        "win": lambda it, h: windowed(it, h, 0),
        "adj": adjoint,
        "rsm": rs_middle,
        "rsc": rs_columns,
        "rsf": rs_finish,
        "win2": lambda it, h: windowed(it, h, 2),
        "upd": update,
    }

    lay_out(0)
    pl.semaphore_wait(barrier, len(greeted))
    signal_round(0, along_x)
    prepared = 0
    for step in ORDER:
        if step == "prep":
            prepare(prepared)
            prepared += 1
            if prepared == 2:
                pl.semaphore_wait(entered.at[0], 3)
                signal_round(1, along_z)
            if prepared == FL:
                pl.semaphore_wait(entered.at[1], 3)
            continue
        name, it, h = step.split()
        it, h = int(it), int(h)
        if name == "ags":
            if h > 0:
                lay_out(h)
            ag_start(it, h)
        else:
            steps[name](it, h)

    for it in range(ITERS):
        for h in range(NC):
            landed(ag.at[it, h, pl.ds(0, NSD - 1)], ag_send.at[it, h])
            landed(part.at[it, h, pl.ds(0, NSD - 1)], rs_send.at[it, h])
            for k in (0, 2):
                field_wait(sfield, it, h, k, a2a_send)
            for k in (1, 3):
                if NW == 1:
                    traces_wait(straces, it, h, k, a2a_send)
                else:
                    pl.when(lane == h // 2)(
                        lambda it=it, h=h, k=k: traces_wait(straces, it, h, k, a2a_send)
                    )


def per_device(reflection, focusing, onsets):
    high, low = tables()
    vmem = pl.BlockSpec(memory_space=pltpu.VMEM)
    block = jax.ShapeDtypeStruct(focusing.shape, F32)
    return pl.pallas_call(
        kernel,
        out_shape=(block, block),
        in_specs=[pl.BlockSpec(memory_space=pl.ANY), vmem, vmem, vmem, vmem],
        out_specs=(vmem, vmem),
        scratch_shapes=[
            pltpu.VMEM((2, 2, LANES, 1024), F32),
            pltpu.VMEM((FL, 2 * LANES, 1024), BF16),
            pltpu.VMEM((FL, 2 * LANES, 1024), BF16),
            pltpu.VMEM((FL, 1024, 2 * LANES), BF16),
            pltpu.VMEM((FL, 1024, 2 * LANES), BF16),
            pltpu.VMEM((ITERS, NC, NSD, ROWS, LANES), F32),
            pltpu.VMEM((ITERS, NC, NSD, ROWS, LANES), F32),
            pltpu.VMEM((ITERS, NC, 4, HALF, LANES), F32),
            pltpu.VMEM((ITERS, NC, 4, ROWS, LANES), F32),
            pltpu.VMEM((ITERS, NC, ROWS, LANES), F32),
            pltpu.VMEM((ITERS, NC, 2, ROWS, LANES), F32),
            pltpu.VMEM((ITERS, NC, 2, ROWS, LANES), F32),
            pltpu.VMEM((ITERS, NC, 2, TRACES, LANES), F32),
            pltpu.VMEM((ITERS, NC, 2, TRACES, LANES), F32),
            pltpu.SemaphoreType.DMA((2,)),
            pltpu.SemaphoreType.DMA((ITERS, NC, 4)),
            pltpu.SemaphoreType.DMA((ITERS, NC, 4)),
            pltpu.SemaphoreType.DMA((ITERS, NC)),
            pltpu.SemaphoreType.DMA((ITERS, NC, 14)),
            pltpu.SemaphoreType.DMA((ITERS, NC)),
            pltpu.SemaphoreType.DMA((ITERS, NC, 14)),
            pltpu.SemaphoreType.REGULAR((2,)),
        ],
        compiler_params=pltpu.CompilerParams(
            collective_id=0, has_side_effects=True, vmem_limit_bytes=62 * 1024 * 1024
        ),
        name="marchenko",
    )(reflection, focusing, onsets, jnp.asarray(high), jnp.asarray(low))


def solution(mesh):
    placed = (P(None, "freq", "src", None), P(None, "freq", None, "src"), P("freq", "src"))
    return jax.shard_map(
        per_device,
        mesh=mesh,
        in_specs=placed,
        out_specs=(P(None, "freq", None, "src"), P(None, "freq", None, "src")),
        check_vma=False,
    )
```

time: 240 us -> 218 us (0.908)
  Pallas kernels: 235 us -> 213 us
    pallas_call x1, Pallas kernels: 235 us -> 213 us  [per_device(): pl.pallas_call(kernel, out_shape=(block, block), in_specs=[pl.BlockSpec(m...]
where the time goes in v2:
time: 218 us; the launch traced here: 217 us
  Pallas kernels  213 us (98%)
  local copies, waits for them, and re-layouts  3.77 us (2%)
    pallas_call x1, Pallas kernels, per_device(): pl.pallas_call(kernel, out_shape=(block, block), in_specs=[pl.BlockSpec(m...  213 us

profile of v2, /device:TPU:1, one launch (start us, length us, event | category | flops | bytes accessed | tf_op | source)
XLA Modules:
  0.0 217.0 jit_solution(8247150647802150975)
XLA Ops:
  0.6 212.6 %marchenko.1 = (f32[2,8,64,128]{3,2,1,0:T(8,128)}, f32[2,8,64,128]{3,2,1,0:T(8,128)}) custom-call(f32[2,8,128,1024]{3,2,1,0:T(8,128)} %refl.1, f32[2,8,64,128]{3,2,1,0:T(8,128)} %foc.1, s32[2,128]{1,0:T(2,128)} %onsets.1, bf16[512,256]{1,0:T(8,128)(2,1)} %constant.4.clone.th, bf16[512,256]{1,0:T(8,128)(2,1)} %constant.5.clone.tl), custom_call_target="tpu_custom_call" | custom-call | tf_op jit(solution)/shard_map/marchenko/pallas_call | solution.py:448
  213.2 1.9 copy.9
  215.1 1.9 copy.10

commit v3 on v2

--- a/solution.py
+++ b/solution.py
@@ -26,18 +26,18 @@
 LANES = 128
 NF = 256
 ORDER = (
-    "ags 0 0", "ags 0 1", "prep", "prep", "prep", "prep", "agz 0 0", "prep", "prep", "agz 0 1",
-    "prep", "prep", "agy 0 0", "ags 0 2", "ags 0 3", "agy 0 1", "agz 0 2", "agf 0 0", "fwd 0 0",
-    "agz 0 3", "win 0 0", "agf 0 1", "fwd 0 1", "agy 0 2", "agy 0 3", "adj 0 0", "win 0 1",
-    "agf 0 2", "fwd 0 2", "rsm 0 0", "agf 0 3", "fwd 0 3", "adj 0 1", "rsc 0 0", "win 0 2",
-    "win 0 3", "rsm 0 1", "rsf 0 0", "adj 0 2", "rsc 0 1", "adj 0 3", "win2 0 0", "rsm 0 2",
-    "rsf 0 1", "rsm 0 3", "upd 0 0", "agz 1 0", "win2 0 1", "rsc 0 2", "rsc 0 3", "upd 0 1",
-    "agz 1 1", "agy 1 0", "rsf 0 2", "rsf 0 3", "agy 1 1", "win2 0 2", "agf 1 0", "fwd 1 0",
-    "win2 0 3", "agf 1 1", "fwd 1 1", "upd 0 2", "agz 1 2", "win 1 0", "upd 0 3", "agz 1 3",
-    "agy 1 2", "win 1 1", "agy 1 3", "adj 1 0", "agf 1 2", "fwd 1 2", "agf 1 3", "fwd 1 3",
-    "rsm 1 0", "adj 1 1", "win 1 2", "rsc 1 0", "win 1 3", "rsm 1 1", "adj 1 2", "rsf 1 0",
-    "rsc 1 1", "adj 1 3", "win2 1 0", "rsm 1 2", "rsf 1 1", "rsm 1 3", "upd 1 0", "rsc 1 2",
-    "win2 1 1", "rsc 1 3", "rsf 1 2", "upd 1 1", "rsf 1 3", "win2 1 2", "win2 1 3", "upd 1 2",
+    "ags 0 0", "ags 0 1", "prep", "prep", "prep", "prep", "prep", "agz 0 0", "prep", "agy 0 0",
+    "prep", "prep", "ags 0 2", "agz 0 1", "agf 0 0", "fwd 0 0", "agy 0 1", "agz 0 2", "ags 0 3",
+    "agf 0 1", "fwd 0 1", "agy 0 2", "agz 0 3", "win 0 0", "agf 0 2", "fwd 0 2", "agy 0 3",
+    "win 0 1", "adj 0 0", "agf 0 3", "fwd 0 3", "rsm 0 0", "win 0 2", "adj 0 1", "rsc 0 0",
+    "win 0 3", "rsm 0 1", "rsf 0 0", "adj 0 2", "rsc 0 1", "rsm 0 2", "rsf 0 1", "win2 0 0",
+    "rsc 0 2", "adj 0 3", "win2 0 1", "rsm 0 3", "rsf 0 2", "upd 0 0", "upd 0 1", "rsc 0 3",
+    "win2 0 2", "agz 1 1", "agy 1 1", "agz 1 0", "rsf 0 3", "agf 1 1", "fwd 1 1", "agy 1 0",
+    "upd 0 2", "agf 1 0", "win2 0 3", "fwd 1 0", "agz 1 2", "agy 1 2", "win 1 1", "upd 0 3",
+    "agf 1 2", "fwd 1 2", "agz 1 3", "win 1 0", "agy 1 3", "adj 1 1", "agf 1 3", "fwd 1 3",
+    "rsm 1 1", "win 1 2", "adj 1 0", "rsc 1 1", "win 1 3", "rsm 1 0", "rsf 1 1", "adj 1 2",
+    "rsc 1 0", "rsf 1 0", "rsm 1 2", "adj 1 3", "rsc 1 2", "win2 1 1", "rsm 1 3", "rsf 1 2",
+    "rsc 1 3", "rsf 1 3", "win2 1 2", "win2 1 0", "upd 1 1", "win2 1 3", "upd 1 2", "upd 1 0",
     "upd 1 3",
 )
 MESH = pl.DeviceIdType.MESH
@@ -64,7 +64,7 @@
 
 
 def kernel(
-    refl, foc, onsets, th, tl, down_out, up_out,
+    refl, foc, onsets, th, tl, out,
     rstage, rhi, rlo, thi, tlo, ag, part, r1, r2, rz, sfield, rfield, straces, rtraces,
     stage_sem, a2a_send, a2a_recv, ag_send, ag_recv, rs_send, rs_recv, entered,
 ):
@@ -371,21 +371,18 @@
         for c in range(2):
             for f in range(FL):
                 rows = slice(f * FROWS + c * NQ, f * FROWS + (c + 1) * NQ)
-                field = (
-                    ag[0, h, src, rows, :]
-                    - rfield[it, h, 1, pl.ds(c * FL + f, NQ, stride=MSG), :]
-                )
+                field = rfield[it, h, 1, pl.ds(c * FL + f, NQ, stride=MSG), :]
                 if it + 1 < ITERS:
-                    ag[it + 1, h, src, rows, :] = field
+                    ag[it + 1, h, src, rows, :] = ag[0, h, src, rows, :] - field
                 else:
-                    down_out[c, f, pl.ds(h, NQ, stride=NC), :] = field
+                    out[0, c, f, pl.ds(h, NQ, stride=NC), :] = field
         if it + 1 < ITERS:
             ag_start(it + 1, h)
 
     def write_upgoing(h):
         for c in range(2):
             for f in range(FL):
-                up_out[c, f, pl.ds(h, NQ, stride=NC), :] = rfield[
+                out[1, c, f, pl.ds(h, NQ, stride=NC), :] = rfield[
                     ITERS - 1, h, 0, pl.ds(c * FL + f, NQ, stride=MSG), :
                 ]
 
@@ -444,12 +441,11 @@
 def per_device(reflection, focusing, onsets):
     high, low = tables()
     vmem = pl.BlockSpec(memory_space=pltpu.VMEM)
-    block = jax.ShapeDtypeStruct(focusing.shape, F32)
-    return pl.pallas_call(
+    fields = pl.pallas_call(
         kernel,
-        out_shape=(block, block),
+        out_shape=jax.ShapeDtypeStruct((2, *focusing.shape), F32),
         in_specs=[pl.BlockSpec(memory_space=pl.ANY), vmem, vmem, vmem, vmem],
-        out_specs=(vmem, vmem),
+        out_specs=vmem,
         scratch_shapes=[
             pltpu.VMEM((2, 2, LANES, 1024), F32),
             pltpu.VMEM((FL, 2 * LANES, 1024), BF16),
@@ -479,6 +475,7 @@
         ),
         name="marchenko",
     )(reflection, focusing, onsets, jnp.asarray(high), jnp.asarray(low))
+    return focusing - fields[0], fields[1]
 
 
 def solution(mesh):

time: 218 us -> 199 us (0.913)
  Pallas kernels: 213 us -> 194 us
    pallas_call x1, Pallas kernels: 213 us -> 194 us  [per_device(): pl.pallas_call(kernel, out_shape=jax.ShapeDtypeStruct((2, *focusing.shape...]
    unnamed x2, local copies, waits for them, and re-layouts: 3.77 us -> 0.01 us
where the time goes in v3:
time: 199 us
  Pallas kernels  194 us (97%)
    pallas_call x1, Pallas kernels, per_device(): pl.pallas_call(kernel, out_shape=jax.ShapeDtypeStruct((2, *focusing.shape...  194 us

profile of v3, /device:TPU:1, one launch (start us, length us, event | category | flops | bytes accessed | tf_op | source)
XLA Modules:
  0.0 198.6 jit_solution(17245025801635057542)
XLA Ops:
  0.6 0.0 copy-start
  0.6 194.2 %marchenko.1 = f32[2,2,8,64,128]{4,3,2,1,0:T(8,128)} custom-call(f32[2,8,128,1024]{3,2,1,0:T(8,128)} %refl.1, f32[2,8,64,128]{3,2,1,0:T(8,128)} %foc.1, s32[2,128]{1,0:T(2,128)} %onsets.1, bf16[512,256]{1,0:T(8,128)(2,1)} %constant.4.clone.th, bf16[512,256]{1,0:T(8,128)(2,1)} %constant.5.clone.tl), custom_call_target="tpu_custom_call" | custom-call | tf_op jit(solution)/shard_map/marchenko/pallas_call | solution.py:444
  194.8 1.9 slice_bitcast_fusion
  196.7 0.0 copy-done
  196.7 1.9 bitcast_subtract_fusion
Async XLA Ops:
  0.6 196.1 %copy-start = (f32[2,8,64,128]{3,2,1,0:T(8,128)S(1)}, f32[2,8,64,128]{3,2,1,0:T(8,128)}, u32[]{:S(2)}) copy-start(f32[2,8,64,128]{3,2,1,0:T(8,128)} %foc.1) | copy-start | bytes 1572868

commit v4 on v3

--- a/solution.py
+++ b/solution.py
@@ -26,19 +26,19 @@
 LANES = 128
 NF = 256
 ORDER = (
-    "ags 0 0", "ags 0 1", "prep", "prep", "prep", "prep", "prep", "agz 0 0", "prep", "agy 0 0",
-    "prep", "prep", "ags 0 2", "agz 0 1", "agf 0 0", "fwd 0 0", "agy 0 1", "agz 0 2", "ags 0 3",
-    "agf 0 1", "fwd 0 1", "agy 0 2", "agz 0 3", "win 0 0", "agf 0 2", "fwd 0 2", "agy 0 3",
-    "win 0 1", "adj 0 0", "agf 0 3", "fwd 0 3", "rsm 0 0", "win 0 2", "adj 0 1", "rsc 0 0",
-    "win 0 3", "rsm 0 1", "rsf 0 0", "adj 0 2", "rsc 0 1", "rsm 0 2", "rsf 0 1", "win2 0 0",
-    "rsc 0 2", "adj 0 3", "win2 0 1", "rsm 0 3", "rsf 0 2", "upd 0 0", "upd 0 1", "rsc 0 3",
-    "win2 0 2", "agz 1 1", "agy 1 1", "agz 1 0", "rsf 0 3", "agf 1 1", "fwd 1 1", "agy 1 0",
-    "upd 0 2", "agf 1 0", "win2 0 3", "fwd 1 0", "agz 1 2", "agy 1 2", "win 1 1", "upd 0 3",
-    "agf 1 2", "fwd 1 2", "agz 1 3", "win 1 0", "agy 1 3", "adj 1 1", "agf 1 3", "fwd 1 3",
-    "rsm 1 1", "win 1 2", "adj 1 0", "rsc 1 1", "win 1 3", "rsm 1 0", "rsf 1 1", "adj 1 2",
-    "rsc 1 0", "rsf 1 0", "rsm 1 2", "adj 1 3", "rsc 1 2", "win2 1 1", "rsm 1 3", "rsf 1 2",
-    "rsc 1 3", "rsf 1 3", "win2 1 2", "win2 1 0", "upd 1 1", "win2 1 3", "upd 1 2", "upd 1 0",
-    "upd 1 3",
+    "ags 0 1", "ags 0 0", "prep", "prep", "prep", "prep", "agz 0 1", "prep", "agz 0 0",
+    "agy 0 0", "agy 0 1", "ags 0 2", "ags 0 3", "prep", "prep", "prep", "agz 0 2", "agf 0 0",
+    "fwd 0 0", "agf 0 1", "fwd 0 1", "win 0 0", "agy 0 2", "agz 0 3", "win 0 1", "agf 0 2",
+    "fwd 0 2", "agy 0 3", "adj 0 0", "agf 0 3", "fwd 0 3", "rsm 0 0", "adj 0 1", "win 0 2",
+    "rsc 0 0", "win 0 3", "rsm 0 1", "rsf 0 0", "adj 0 2", "rsc 0 1", "rsm 0 2", "rsf 0 1",
+    "win2 0 0", "adj 0 3", "rsc 0 2", "win2 0 1", "rsm 0 3", "rsf 0 2", "upd 0 0", "rsc 0 3",
+    "agz 1 0", "win2 0 2", "agy 1 0", "upd 0 1", "agf 1 0", "rsf 0 3", "fwd 1 0", "agz 1 1",
+    "upd 0 2", "agy 1 1", "win2 0 3", "agz 1 2", "win 1 0", "agf 1 1", "fwd 1 1", "agy 1 2",
+    "upd 0 3", "agf 1 2", "fwd 1 2", "agz 1 3", "win 1 1", "agy 1 3", "adj 1 0", "agf 1 3",
+    "fwd 1 3", "win 1 2", "rsm 1 0", "adj 1 1", "rsc 1 0", "win 1 3", "rsm 1 1", "adj 1 2",
+    "rsf 1 0", "rsc 1 1", "rsm 1 2", "adj 1 3", "rsf 1 1", "rsc 1 2", "win2 1 0", "rsm 1 3",
+    "rsf 1 2", "rsc 1 3", "rsf 1 3", "upd 1 0", "win2 1 2", "win2 1 1", "win2 1 3", "upd 1 2",
+    "upd 1 1", "upd 1 3",
 )
 MESH = pl.DeviceIdType.MESH
 F32 = jnp.float32

time: 199 us -> 197 us (0.990)
  Pallas kernels: 194 us -> 192 us
    pallas_call x1, Pallas kernels: 194 us -> 192 us  [per_device(): pl.pallas_call(kernel, out_shape=jax.ShapeDtypeStruct((2, *focusing.shape...]
where the time goes in v4:
time: 197 us; the launch traced here: 196 us
  Pallas kernels  192 us (97%)
    pallas_call x1, Pallas kernels, per_device(): pl.pallas_call(kernel, out_shape=jax.ShapeDtypeStruct((2, *focusing.shape...  192 us

profile of v4, /device:TPU:1, one launch (start us, length us, event | category | flops | bytes accessed | tf_op | source)
XLA Modules:
  0.0 196.0 jit_solution(18120406013069930620)
XLA Ops:
  0.6 0.0 copy-start
  0.6 191.6 %marchenko.1 = f32[2,2,8,64,128]{4,3,2,1,0:T(8,128)} custom-call(f32[2,8,128,1024]{3,2,1,0:T(8,128)} %refl.1, f32[2,8,64,128]{3,2,1,0:T(8,128)} %foc.1, s32[2,128]{1,0:T(2,128)} %onsets.1, bf16[512,256]{1,0:T(8,128)(2,1)} %constant.4.clone.th, bf16[512,256]{1,0:T(8,128)(2,1)} %constant.5.clone.tl), custom_call_target="tpu_custom_call" | custom-call | tf_op jit(solution)/shard_map/marchenko/pallas_call | solution.py:444
  192.2 1.9 slice_bitcast_fusion
  194.1 0.0 copy-done
  194.1 1.9 bitcast_subtract_fusion
Async XLA Ops:
  0.6 193.5 %copy-start = (f32[2,8,64,128]{3,2,1,0:T(8,128)S(1)}, f32[2,8,64,128]{3,2,1,0:T(8,128)}, u32[]{:S(2)}) copy-start(f32[2,8,64,128]{3,2,1,0:T(8,128)} %foc.1) | copy-start | bytes 1572868
